TPU v7x, 32 devices: a whole 2x2x4 slice. The times are simulated.
32 devices in a mesh: req: 16 (over z, y, x), tp: 2 (over core).
Axes of the slice: x: 2, y: 2, z: 4, core: 2. Of those that a mesh axis runs over, the one named last changes fastest.
Arguments:
- residual: bfloat16 [512, 2048], P('req'), may hold values from -6 to 6
- fresh_qkv: bfloat16 [512, 3, 2048], P('req', None, 'tp'), may hold values from -32 to 32
- kv_cache: bfloat16 [512, 24, 2, 2048], P('req', None, None, 'tp'), may hold values from -32 to 32
- cache_len: int32 [512], P('req'), may hold values from 2 to 24, as said below
- out_proj: bfloat16 [2048, 2048], P('tp'), may hold values from -0.125 to 0.125
- norm_gain: float32 [2048], replicated, may hold values from 0.1 to 1.9
- router_weight: float32 [2048, 16], replicated, may hold values from -7.9549513 to 7.9549513
- expert_ids: int32 [512, 8], P('req'), may hold values from 0 to 15, all different within a row; in each aligned block of 32 rows (0 to 31, 32 to 63, ...) at most 32 rows name the same one
- gate_up: bfloat16 [16, 2048, 2, 1024], P('req', None, None, 'tp'), may hold values from -0.125 to 0.125
- down_proj: bfloat16 [16, 1024, 2048], P('req', 'tp'), may hold values from -0.1875 to 0.1875
Outputs:
- layer_out: bfloat16 [512, 2048], P('req', 'tp')
Inputs may be any that keep to these rules, and one draw needn't show every extreme that they name: `expert_ids`: each row names 8 different experts; among the 32 rows of one device no expert is named by more than 32 rows, and some device reaches 32. `cache_len`: some request uses all 24 positions.
All inputs are finite; a program needn't handle non-finite values.
Results may differ from a plain program's by a relative error of at most 0.018.
Values may be sent and summed in bfloat16 or wider, within the bound.
A program may use at most 128 MiB of HBM per device.

v0:
```python
import jax
import jax.numpy as jnp
from jax import lax
from jax.sharding import PartitionSpec as P

HD = 128
TOP = 8


def rms_normed(hidden_in, gain):
    values = hidden_in.astype(jnp.float32)
    scale_inv = lax.rsqrt(jnp.mean(values * values, axis=-1, keepdims=True) + 1e-05)
    return (values * scale_inv * gain).astype(jnp.bfloat16)


def expert_part(slots_in, gate_up, down_proj):
    layout = slots_in.shape
    flat_in = slots_in.reshape(-1, layout[-1])
    units_here = down_proj.shape[1]
    both = jnp.dot(
        flat_in, gate_up[0].reshape(layout[-1], 2 * units_here), preferred_element_type=jnp.float32
    )
    both = both.reshape(-1, 2, units_here)
    inner = (jax.nn.silu(both[:, 0]) * both[:, 1]).astype(jnp.bfloat16)
    result = jnp.dot(inner, down_proj[0], preferred_element_type=jnp.float32)
    return result.reshape(layout[:-1] + (down_proj.shape[2],))


def send_back(results):
    return lax.all_to_all(results, "req", split_axis=0, concat_axis=0, tiled=True)


def local(
    residual,
    fresh_qkv,
    kv_cache,
    cache_len,
    out_proj,
    norm_gain,
    router_weight,
    expert_ids,
    gate_up,
    down_proj,
):
    requests = residual.shape[0]
    tp_place = lax.axis_index("tp")
    experts = lax.axis_size("req")
    capacity = 2 * requests * TOP // experts
    local_heads = fresh_qkv.shape[2] // HD
    ctx_len = kv_cache.shape[1]
    queries = fresh_qkv[:, 0].reshape(requests, local_heads, HD)
    new_keys = fresh_qkv[:, 1].reshape(requests, local_heads, HD)
    new_values = fresh_qkv[:, 2].reshape(requests, local_heads, HD)
    cache_keys = kv_cache[:, :, 0].reshape(requests, ctx_len, local_heads, HD)
    cache_values = kv_cache[:, :, 1].reshape(requests, ctx_len, local_heads, HD)
    factor = HD ** (-0.5)
    scores = (
        jnp.einsum("nhd,nchd->nhc", queries, cache_keys, preferred_element_type=jnp.float32)
        * factor
    )
    own_score = (
        jnp.einsum("nhd,nhd->nh", queries, new_keys, preferred_element_type=jnp.float32) * factor
    )
    valid = (jnp.arange(ctx_len, dtype=jnp.int32)[None, :] < cache_len[:, None])[:, None, :]
    masked = jnp.where(valid, scores, -jnp.inf)
    top_score = jnp.maximum(jnp.max(masked, axis=-1), own_score)
    expos = jnp.where(valid, jnp.exp(masked - top_score[..., None]), 0.0)
    own_expo = jnp.exp(own_score - top_score)
    total = jnp.sum(expos, axis=-1) + own_expo
    weights = (expos / total[..., None]).astype(jnp.bfloat16)
    own_weight = (own_expo / total).astype(jnp.bfloat16)
    mixed = jnp.einsum("nhc,nchd->nhd", weights, cache_values, preferred_element_type=jnp.float32)
    mixed = mixed + own_weight.astype(jnp.float32)[..., None] * new_values.astype(jnp.float32)
    attended = mixed.astype(jnp.bfloat16).reshape(requests, local_heads * HD)
    partial_value = jnp.dot(attended, out_proj, preferred_element_type=jnp.float32)
    summed = lax.psum(partial_value, "tp")
    hidden = (residual.astype(jnp.float32) + summed).astype(jnp.bfloat16)
    normed = rms_normed(hidden, norm_gain)
    logits = jnp.dot(normed.astype(jnp.float32), router_weight, precision=lax.Precision.HIGHEST)
    chosen = jnp.take_along_axis(logits, expert_ids, axis=1)
    gate_vals = jax.nn.softmax(chosen, axis=-1)
    flat_ids = expert_ids.reshape(-1)
    onehot = (flat_ids[:, None] == jnp.arange(experts, dtype=jnp.int32)[None, :]).astype(jnp.int32)
    running = jnp.cumsum(onehot, axis=0)
    slot_index = jnp.sum(running * onehot, axis=1) - 1
    position = flat_ids * capacity + slot_index
    selector = (
        position[None, :] == jnp.arange(experts * capacity, dtype=jnp.int32)[:, None]
    ).astype(jnp.float32)
    selector = selector.reshape(experts * capacity, requests, TOP)
    picker = jnp.sum(selector, axis=-1).astype(jnp.bfloat16)
    outgoing = jnp.dot(picker, normed, preferred_element_type=jnp.float32).astype(jnp.bfloat16)
    outgoing = outgoing.reshape(experts, capacity, normed.shape[1])
    combiner = jnp.sum(selector * gate_vals[None, :, :], axis=-1)
    returned = send_back(
        expert_part(
            lax.all_to_all(outgoing, "req", split_axis=0, concat_axis=0, tiled=True),
            gate_up,
            down_proj,
        )
    )
    moe_sum = jnp.dot(
        combiner.T,
        returned.reshape(experts * capacity, -1),
        precision=lax.Precision.HIGHEST,
        preferred_element_type=jnp.float32,
    )
    moe_share = lax.psum_scatter(moe_sum, "tp", scatter_dimension=1, tiled=True)
    width_here = moe_share.shape[1]
    own_cols = lax.dynamic_slice_in_dim(hidden, tp_place * width_here, width_here, 1)
    return (own_cols.astype(jnp.float32) + moe_share).astype(jnp.bfloat16)


def solution(mesh):
    in_specs = (
        P("req", None),
        P("req", None, "tp"),
        P("req", None, None, "tp"),
        P("req"),
        P("tp", None),
        P(),
        P(),
        P("req", None),
        P("req", None, None, "tp"),
        P("req", "tp", None),
    )
    out_specs = P("req", "tp")
    return jax.shard_map(local, mesh=mesh, in_specs=in_specs, out_specs=out_specs, check_vma=False)
```

profile of v0, /device:TPU:0, one launch (start us, length us, event | category | flops | bytes accessed | tf_op | source)
XLA Modules:
  0.0 238.4 jit_solution(5250030907298059460)
XLA Ops:
  6.5 1.1 convert_bitcast_fusion
  7.7 0.1 fusion.14
  7.9 17.1 %slice_reduce_fusion = (bf16[32,24,1024]{2,1,0:T(8,128)(2,1)}, bf16[32,24,1024]{2,1,0:T(8,128)(2,1)S(1)}) fusion(bf16[32,24,2,1024]{3,2,1,0:T(2,128)(2,1)} %param.12), kind=kLoop, calls=%fused_computation.1 | loop fusion | bytes 6291456 | tf_op jit(solution)/shard_map/slice | solution.py:55
  25.1 0.9 fusion.5
  26.0 0.1 copy.33
  26.3 0.2 copy.38
  26.5 2.0 fusion.2
  28.5 0.1 fusion.13
  28.7 3.8 %fusion.18 = f32[32,2048]{1,0:T(8,128)} fusion(bf16[1024,2048]{1,0:T(8,128)(2,1)} %param.14, bf16[4,8,8,128]{3,2,1,0:T(8,128)(2,1)S(1)} %bitcast.109), kind=kOutput, calls=%fused_computation.36 | convolution fusion | flops 134217728 | bytes 4521984 | tf_op jit(solution)/shard_map/dot_general | solution.py:75
  32.8 0.6 reduce-window.6
  33.4 0.2 slice_reduce_fusion.2
  33.8 0.1 reshape.124
  33.9 19.7 %all-reduce.2.cloned.1.call-done = f32[32,2048]{1,0:T(8,128)} async-done(((f32[32,2048]{1,0:T(8,128)}), f32[32,2048]{1,0:T(8,128)}) %all-reduce.2.cloned.1.call-update) | async-done | bytes 262160 | tf_op jit(solution)/shard_map/psum | solution.py:76
  53.6 1.1 fusion.9
  54.8 0.2 fusion.23
  55.0 2.1 gather_fusion
  57.2 0.1 fusion.33
  57.3 0.2 fusion.30
  57.6 0.4 convert_reduce_fusion
  58.0 2.1 convolution_convert_fusion
  60.0 6.8 %all-to-all-start = ((bf16[16,32,2048]{2,1,0:T(8,128)(2,1)}), bf16[16,32,2048]{2,1,0:T(8,128)(2,1)}, u32[]{:S(2)}, u32[]{:S(2)}) async-start(bf16[16,32,2048]{2,1,0:T(8,128)(2,1)} %bitcast.105), calls=%async_computation | async-start | bytes 4194304 | tf_op jit(solution)/shard_map/all_to_all | solution.py:97
  66.9 0.2 reduce-scatter.2.cloned.1.call-start
  67.1 5.3 %copy.49 = bf16[256,8,2,512]{3,1,2,0:T(8,128)(2,1)} copy(bf16[256,8,2,512]{3,2,1,0:T(2,128)(2,1)} %bitcast.106) | data formatting | bytes 8388608
  72.5 6.5 %copy.30 = bf16[1024,2048]{1,0:T(8,128)(2,1)} copy(bf16[1024,2048]{0,1:T(8,128)(2,1)} %bitcast.104) | data formatting | bytes 8388608 | tf_op jit(solution)/shard_map/dot_general | solution.py:20
  78.9 31.2 %all-to-all-done = bf16[16,32,2048]{2,1,0:T(8,128)(2,1)} async-done(((bf16[16,32,2048]{2,1,0:T(8,128)(2,1)}), bf16[16,32,2048]{2,1,0:T(8,128)(2,1)}, u32[]{:S(2)}, u32[]{:S(2)}) %all-to-all-start) | async-done | bytes 2097184 | tf_op jit(solution)/shard_map/all_to_all | solution.py:97
  110.1 5.2 %fusion.34 = f32[512,2,512]{2,0,1:T(8,128)S(1)} fusion(bf16[512,2048,1]{1,0,2:T(8,128)(2,1)} %bitcast.8, bf16[2,512,2048]{2,1,0:T(8,128)(2,1)} %bitcast.107), kind=kOutput, calls=%fused_computation.68 | convolution fusion | flops 2147483648 | bytes 8388608 | tf_op jit(solution)/shard_map/dot_general | solution.py:20
  115.3 0.3 fusion.8
  115.7 1.3 fusion
  117.0 103.6 %all_to_all.10 = f32[16,32,2048]{2,1,0:T(8,128)S(1)} all-to-all(f32[16,32,2048]{2,1,0:T(8,128)S(1)} %fusion), channel_id=1, replica_groups=mesh['req'=16,'tp'=2] {'req'}, dimensions={0} | all-to-all | bytes 8388608 | tf_op jit(solution)/shard_map/all_to_all | solution.py:30
  220.5 3.2 %fusion.35 = f32[32,2048]{1,0:T(8,128)} fusion(f32[512,32]{0,1:T(8,128)S(1)} %get-tuple-element.8, f32[512,2048]{1,0:T(8,128)S(1)} %bitcast.103), kind=kOutput, calls=%fused_computation.69 | convolution fusion | flops 402653184 | bytes 4521984 | tf_op jit(solution)/shard_map/dot_general | solution.py:102
  223.7 6.3 %reduce-scatter.2.cloned.1.call-done = f32[32,1024]{1,0:T(8,128)} async-done(((f32[32,2048]{1,0:T(8,128)}), f32[32,1024]{1,0:T(8,128)}) %reduce-scatter.2.cloned.1.call-update) | async-done | bytes 131088 | tf_op jit(solution)/shard_map/reduce_scatter | solution.py:108
  230.0 1.6 add_convert_fusion.1
  (41 shorter events, 1.1 us)
Async XLA Ops:
  6.5 109.1 %copy-start = (bf16[1,512,2048]{2,1,0:T(8,128)(2,1)S(1)}, bf16[1,512,2048]{2,1,0:T(8,128)(2,1)}, u32[]{:S(2)}) copy-start(bf16[1,512,2048]{2,1,0:T(8,128)(2,1)} %param.19) | copy-start | bytes 6291460
  6.5 47.1 %all-reduce.2.cloned.1.call-start = ((), (), s32[]{:S(2)}) async-start(), calls=%async_computation.3 | async-start | bytes 524288 | tf_op jit(solution)/shard_map/psum | solution.py:76
  25.1 1.0 copy-start.5
  28.7 3.8 %copy-start.4 = (s32[32,8]{0,1:T(8,128)S(1)}, s32[32,8]{0,1:T(8,128)}, u32[]{:S(2)}) copy-start(s32[32,8]{0,1:T(8,128)} %param.17) | copy-start | bytes 3076
  28.7 25.0 %copy-start.1 = (bf16[32,2048]{1,0:T(8,128)(2,1)S(1)}, bf16[32,2048]{1,0:T(8,128)(2,1)}, u32[]{:S(2)}) copy-start(bf16[32,2048]{1,0:T(8,128)(2,1)} %param.10) | copy-start | bytes 393220
  28.7 26.1 %copy-start.2 = (f32[2048,16]{0,1:T(8,128)S(1)}, f32[2048,16]{0,1:T(8,128)}, u32[]{:S(2)}) copy-start(f32[2048,16]{0,1:T(8,128)} %param.16) | copy-start | bytes 393220
  28.7 26.1 %copy-start.3 = (f32[2048]{0:T(1024)S(1)}, f32[2048]{0:T(1024)}, u32[]{:S(2)}) copy-start(f32[2048]{0:T(1024)} %param.15) | copy-start | bytes 24580
  60.0 50.1 %all-to-all-start = ((bf16[16,32,2048]{2,1,0:T(8,128)(2,1)}), bf16[16,32,2048]{2,1,0:T(8,128)(2,1)}, u32[]{:S(2)}, u32[]{:S(2)}) async-start(bf16[16,32,2048]{2,1,0:T(8,128)(2,1)} %bitcast.105), calls=%async_computation | async-start | bytes 4194304 | tf_op jit(solution)/shard_map/all_to_all | solution.py:97
  66.9 163.1 %reduce-scatter.2.cloned.1.call-start = ((), (), s32[]{:S(2)}) async-start(), calls=%async_computation.4 | async-start | bytes 393216 | tf_op jit(solution)/shard_map/reduce_scatter | solution.py:108
Sparse Core Ops, SparseCore 0:
  32.6 20.9 all-reduce.1
  223.8 6.0 reduce-scatter.1
where the time goes:
time: 239 us; the launch traced here: 238 us
  blocking collectives  104 us (44%)
  waiting for transfers between devices  57.2 us (24%)
  local copies, waits for them, and re-layouts  32.3 us (14%)
  matrix products  18.6 us (8%)
  between operations  13.7 us (6%)
  starting transfers between devices  7.06 us (3%)
  other arithmetic  5.94 us (2%)
    all_to_all x1, blocking collectives, send_back(): lax.all_to_all(results, 'req', split_axis=0, concat_axis=0, tiled=True)  104 us
    all_to_all x1, waiting for transfers between devices, local(): lax.all_to_all(outgoing, 'req', split_axis=0, concat_axis=0, tiled=True)  31.2 us
    psum x1, waiting for transfers between devices, local(): summed = lax.psum(partial_value, 'tp')  19.7 us
    slice x1, local copies, waits for them, and re-layouts, local(): cache_values = kv_cache[:, :, 1].reshape(requests, ctx_len, local_heads, HD)  17.1 us
    all_to_all x1, starting transfers between devices, local(): lax.all_to_all(outgoing, 'req', split_axis=0, concat_axis=0, tiled=True)  6.83 us
    dot_general x1, local copies, waits for them, and re-layouts, expert_part(): jnp.dot(flat_in, gate_up[0].reshape(layout[-1], 2 * units_here), preferre...  6.49 us
    reduce_scatter x1, waiting for transfers between devices, local(): moe_share = lax.psum_scatter(moe_sum, 'tp', scatter_dimension=1, tiled=True)  6.25 us
    unnamed x17, local copies, waits for them, and re-layouts  5.51 us
  transfers between devices with their start and end apart: 3, of which 3 were waited for; matrix products, arithmetic and copies ran while one was open for 6% of the time, Pallas kernels for 0%

commit v1 on v0

--- a/solution.py
+++ b/solution.py
@@ -73,7 +73,7 @@
     mixed = mixed + own_weight.astype(jnp.float32)[..., None] * new_values.astype(jnp.float32)
     attended = mixed.astype(jnp.bfloat16).reshape(requests, local_heads * HD)
     partial_value = jnp.dot(attended, out_proj, preferred_element_type=jnp.float32)
-    summed = lax.psum(partial_value, "tp")
+    summed = jnp.sum(lax.all_gather(partial_value, "tp"), axis=0)
     hidden = (residual.astype(jnp.float32) + summed).astype(jnp.bfloat16)
     normed = rms_normed(hidden, norm_gain)
     logits = jnp.dot(normed.astype(jnp.float32), router_weight, precision=lax.Precision.HIGHEST)

time: 239 us -> 222 us (0.929)
  waiting for transfers between devices: 57.2 us -> 37.5 us
    psum x1 -> x0, waiting for transfers between devices: 19.7 us -> none  [local(): summed = lax.psum(partial_value, 'tp')]
    all_gather x0 -> x1, blocking collectives: none -> 2.39 us  [local(): summed = jnp.sum(lax.all_gather(partial_value, 'tp'), axis=0)]
    unnamed x17 -> x15, local copies, waits for them, and re-layouts: 5.51 us -> 6.34 us
  transfers between devices with their start and end apart: 3 -> 2, of which waited for: 3 -> 2; matrix products, arithmetic and copies ran while one was open for 6% -> 5% of each run, Pallas kernels for 0% -> 0%
where the time goes in v1:
time: 222 us; the launch traced here: 221 us
  blocking collectives  106 us (48%)
  waiting for transfers between devices  37.5 us (17%)
  local copies, waits for them, and re-layouts  33.1 us (15%)
  matrix products  17.9 us (8%)
  between operations  13.7 us (6%)
  starting transfers between devices  8.51 us (4%)
  other arithmetic  4.88 us (2%)
    all_to_all x1, blocking collectives, send_back(): lax.all_to_all(results, 'req', split_axis=0, concat_axis=0, tiled=True)  103 us
    all_to_all x1, waiting for transfers between devices, local(): lax.all_to_all(outgoing, 'req', split_axis=0, concat_axis=0, tiled=True)  31.3 us
    slice x1, local copies, waits for them, and re-layouts, local(): cache_values = kv_cache[:, :, 1].reshape(requests, ctx_len, local_heads, HD)  17.1 us
    all_to_all x1, starting transfers between devices, local(): lax.all_to_all(outgoing, 'req', split_axis=0, concat_axis=0, tiled=True)  8.29 us
    dot_general x1, local copies, waits for them, and re-layouts, expert_part(): jnp.dot(flat_in, gate_up[0].reshape(layout[-1], 2 * units_here), preferre...  6.49 us
    unnamed x15, local copies, waits for them, and re-layouts  6.34 us
    reduce_scatter x1, waiting for transfers between devices, local(): moe_share = lax.psum_scatter(moe_sum, 'tp', scatter_dimension=1, tiled=True)  6.24 us
    dot_general x1, matrix products, expert_part(): jnp.dot(flat_in, gate_up[0].reshape(layout[-1], 2 * units_here), preferre...  5.19 us
  transfers between devices with their start and end apart: 2, of which 2 were waited for; matrix products, arithmetic and copies ran while one was open for 5% of the time, Pallas kernels for 0%

profile of v1, /device:TPU:0, one launch (start us, length us, event | category | flops | bytes accessed | tf_op | source)
XLA Modules:
  0.0 221.2 jit_solution(3213221975296991410)
XLA Ops:
  6.5 0.9 copy.23
  7.7 0.6 reduce-window.6
  8.2 0.2 slice_reduce_fusion.2
  8.7 0.9 convert_bitcast_fusion
  9.7 0.1 fusion.14
  9.9 17.1 %slice_reduce_fusion = (bf16[32,24,1024]{2,1,0:T(8,128)(2,1)}, bf16[32,24,1024]{2,1,0:T(8,128)(2,1)S(1)}) fusion(bf16[32,24,2,1024]{3,2,1,0:T(2,128)(2,1)} %param.12), kind=kLoop, calls=%fused_computation.1 | loop fusion | bytes 6291456 | tf_op jit(solution)/shard_map/slice | solution.py:55
  27.0 0.9 fusion.5
  28.0 0.1 copy.33
  28.3 0.2 copy.38
  28.5 2.0 fusion.2
  30.5 0.1 fusion.13
  30.7 3.0 %fusion.18 = f32[32,2048]{1,0:T(8,128)S(1)} fusion(bf16[1024,2048]{1,0:T(8,128)(2,1)} %param.14, bf16[4,8,8,128]{3,2,1,0:T(8,128)(2,1)S(1)} %bitcast.111), kind=kOutput, calls=%fused_computation.36 | convolution fusion | flops 134217728 | bytes 4521984 | tf_op jit(solution)/shard_map/dot_general | solution.py:75
  33.7 2.4 %all-gather = f32[64,2048]{1,0:T(8,128)S(1)} all-gather(f32[32,2048]{1,0:T(8,128)S(1)} %fusion.18), channel_id=2, replica_groups=mesh['req'=16,'tp'=2] {'tp'}, dimensions={0}, use_global_device_ids=true | all-gather | bytes 786432 | tf_op jit(solution)/shard_map/all_gather | solution.py:76
  36.2 0.2 fusion.9
  36.4 0.3 fusion.23
  36.7 2.1 gather_fusion
  38.8 0.1 fusion.33
  39.0 0.2 fusion.30
  39.3 0.4 convert_reduce_fusion
  39.7 2.1 convolution_convert_fusion
  41.7 8.3 %all-to-all-start = ((bf16[16,32,2048]{2,1,0:T(8,128)(2,1)}), bf16[16,32,2048]{2,1,0:T(8,128)(2,1)}, u32[]{:S(2)}, u32[]{:S(2)}) async-start(bf16[16,32,2048]{2,1,0:T(8,128)(2,1)} %bitcast.106), calls=%async_computation | async-start | bytes 4194304 | tf_op jit(solution)/shard_map/all_to_all | solution.py:97
  50.0 0.2 reduce-scatter.2.cloned.1.call-start
  50.2 5.3 %copy.49 = bf16[256,8,2,512]{3,1,2,0:T(8,128)(2,1)} copy(bf16[256,8,2,512]{3,2,1,0:T(2,128)(2,1)} %bitcast.107) | data formatting | bytes 8388608
  55.6 6.5 %copy.30 = bf16[1024,2048]{1,0:T(8,128)(2,1)} copy(bf16[1024,2048]{0,1:T(8,128)(2,1)} %bitcast.105) | data formatting | bytes 8388608 | tf_op jit(solution)/shard_map/dot_general | solution.py:20
  62.1 31.3 %all-to-all-done = bf16[16,32,2048]{2,1,0:T(8,128)(2,1)} async-done(((bf16[16,32,2048]{2,1,0:T(8,128)(2,1)}), bf16[16,32,2048]{2,1,0:T(8,128)(2,1)}, u32[]{:S(2)}, u32[]{:S(2)}) %all-to-all-start) | async-done | bytes 2097184 | tf_op jit(solution)/shard_map/all_to_all | solution.py:97
  93.3 5.2 %fusion.34 = f32[512,2,512]{2,0,1:T(8,128)S(1)} fusion(bf16[512,2048,1]{1,0,2:T(8,128)(2,1)} %bitcast.9, bf16[2,512,2048]{2,1,0:T(8,128)(2,1)} %bitcast.108), kind=kOutput, calls=%fused_computation.68 | convolution fusion | flops 2147483648 | bytes 8388608 | tf_op jit(solution)/shard_map/dot_general | solution.py:20
  98.5 0.3 fusion.8
  98.9 1.3 fusion
  100.2 103.2 %all_to_all.10 = f32[16,32,2048]{2,1,0:T(8,128)S(1)} all-to-all(f32[16,32,2048]{2,1,0:T(8,128)S(1)} %fusion), channel_id=1, replica_groups=mesh['req'=16,'tp'=2] {'req'}, dimensions={0} | all-to-all | bytes 8388608 | tf_op jit(solution)/shard_map/all_to_all | solution.py:30
  203.4 3.2 %fusion.35 = f32[32,2048]{1,0:T(8,128)} fusion(f32[512,32]{0,1:T(8,128)S(1)} %get-tuple-element.8, f32[512,2048]{1,0:T(8,128)S(1)} %bitcast.104), kind=kOutput, calls=%fused_computation.69 | convolution fusion | flops 402653184 | bytes 4521984 | tf_op jit(solution)/shard_map/dot_general | solution.py:102
  206.6 6.2 %reduce-scatter.2.cloned.1.call-done = f32[32,1024]{1,0:T(8,128)} async-done(((f32[32,2048]{1,0:T(8,128)}), f32[32,1024]{1,0:T(8,128)}) %reduce-scatter.2.cloned.1.call-update) | async-done | bytes 131088 | tf_op jit(solution)/shard_map/reduce_scatter | solution.py:108
  212.8 1.6 add_convert_fusion.1
  (38 shorter events, 1.1 us)
Async XLA Ops:
  6.5 92.3 %copy-start = (bf16[1,512,2048]{2,1,0:T(8,128)(2,1)S(1)}, bf16[1,512,2048]{2,1,0:T(8,128)(2,1)}, u32[]{:S(2)}) copy-start(bf16[1,512,2048]{2,1,0:T(8,128)(2,1)} %param.19) | copy-start | bytes 6291460
  27.0 1.0 copy-start.4
  30.7 5.5 %copy-start.1 = (bf16[32,2048]{1,0:T(8,128)(2,1)S(1)}, bf16[32,2048]{1,0:T(8,128)(2,1)}, u32[]{:S(2)}) copy-start(bf16[32,2048]{1,0:T(8,128)(2,1)} %param.10) | copy-start | bytes 393220
  33.7 2.7 %copy-start.2 = (f32[2048,16]{0,1:T(8,128)S(1)}, f32[2048,16]{0,1:T(8,128)}, u32[]{:S(2)}) copy-start(f32[2048,16]{0,1:T(8,128)} %param.16) | copy-start | bytes 393220
  33.7 2.7 %copy-start.3 = (f32[2048]{0:T(1024)S(1)}, f32[2048]{0:T(1024)}, u32[]{:S(2)}) copy-start(f32[2048]{0:T(1024)} %param.15) | copy-start | bytes 24580
  41.7 51.6 %all-to-all-start = ((bf16[16,32,2048]{2,1,0:T(8,128)(2,1)}), bf16[16,32,2048]{2,1,0:T(8,128)(2,1)}, u32[]{:S(2)}, u32[]{:S(2)}) async-start(bf16[16,32,2048]{2,1,0:T(8,128)(2,1)} %bitcast.106), calls=%async_computation | async-start | bytes 4194304 | tf_op jit(solution)/shard_map/all_to_all | solution.py:97
  50.0 162.8 %reduce-scatter.2.cloned.1.call-start = ((), (), s32[]{:S(2)}) async-start(), calls=%async_computation.3 | async-start | bytes 393216 | tf_op jit(solution)/shard_map/reduce_scatter | solution.py:108
Sparse Core Ops, SparseCore 0:
  206.7 6.0 reduce-scatter.1
